TPU v7x, 512 devices: a whole 4x8x8 slice. The times are simulated.
512 devices in a mesh: patch: 32 (over z_hi, x, core), uly: 16 (over z_lo, y).
Axes of the slice: x: 4, y: 8, z: 8 (z_hi: 4, z_lo: 2; z = z_hi * 2 + z_lo), core: 2. Of those that a mesh axis runs over, the one named last changes fastest.
Arguments:
- queries: bfloat16 [8192, 6144], P(('patch', 'uly')), may hold values from -18 to 18
- keys: bfloat16 [8192, 6144], P(('patch', 'uly')), may hold values from -18 to 18
- values: bfloat16 [8192, 6144], P(('patch', 'uly')), may hold values from -12 to 12
- stale_cache: bfloat16 [2, 8192, 6144], P(None, 'patch', 'uly'), may hold values from -14 to 14
Outputs:
- attended: bfloat16 [8192, 6144], P(('patch', 'uly'))
- fresh_cache: bfloat16 [2, 8192, 6144], P(None, 'patch', 'uly')
All inputs are finite; a program needn't handle non-finite values.
Results may differ from a plain program's by a relative error of at most 0.0055.
Values may be sent and summed in bfloat16 or wider, within the bound.
A program may use at most 128 MiB of HBM per device.

v0:
```python
import jax
import jax.numpy as jnp
from jax import lax
from jax.sharding import PartitionSpec as P

HEADS = 48
HEAD_DIM = 128


def block_length(key_count):
    block_rows = min(key_count, 2048)
    while key_count % block_rows:
        block_rows = block_rows - 1
    return block_rows


def own_attention(query_heads, key_heads, value_heads, score_scale):
    scores = (
        jnp.einsum("qhd,khd->hqk", query_heads, key_heads, preferred_element_type=jnp.float32)
        * score_scale
    )
    peak_value = jnp.max(scores, axis=2)
    weights = jnp.exp(scores - peak_value[:, :, None])
    totals = jnp.sum(weights, axis=2)
    numerators = jnp.einsum(
        "hqk,khd->qhd",
        weights.astype(jnp.bfloat16),
        value_heads,
        preferred_element_type=jnp.float32,
    )
    return (peak_value.T, totals.T, numerators)


def local(queries, keys, values, stale_cache):
    tok_rows, width = queries.shape
    uly_count = lax.axis_size("uly")
    heads_here = HEADS // uly_count
    score_scale = HEAD_DIM ** (-0.5)
    patch_rows = tok_rows * uly_count

    def by_group(matrix):
        return matrix.reshape(tok_rows, uly_count, heads_here, HEAD_DIM)

    query_part, key_part, value_part = (
        lax.all_to_all(by_group(queries), "uly", split_axis=1, concat_axis=0, tiled=True),
        lax.all_to_all(by_group(keys), "uly", split_axis=1, concat_axis=0, tiled=True),
        lax.all_to_all(by_group(values), "uly", split_axis=1, concat_axis=0, tiled=True),
    )
    query_heads = query_part[:, 0]
    key_heads = key_part[:, 0]
    value_heads = value_part[:, 0]
    peak_rows, total_rows, numerators = own_attention(
        query_heads, key_heads, value_heads, score_scale
    )
    own_first = lax.axis_index("patch") * patch_rows

    def update(running, key_block, value_block, begin_row):
        peak_value, totals, numerators_now = running
        scores = (
            jnp.einsum("qhd,khd->hqk", query_heads, key_block, preferred_element_type=jnp.float32)
            * score_scale
        )
        positions = begin_row + lax.iota(jnp.int32, key_block.shape[0])
        own_rows = (positions >= own_first) & (positions < own_first + patch_rows)
        scores = jnp.where(own_rows[None, None, :], -1e30, scores)
        new_peak = jnp.maximum(peak_value, jnp.max(scores, axis=2))
        shrink = jnp.exp(peak_value - new_peak)
        weights = jnp.exp(scores - new_peak[:, :, None])
        totals = totals * shrink + jnp.sum(weights, axis=2)
        numerators_now = numerators_now * shrink.T[:, :, None] + jnp.einsum(
            "hqk,khd->qhd",
            weights.astype(jnp.bfloat16),
            value_block,
            preferred_element_type=jnp.float32,
        )
        return (new_peak, totals, numerators_now)

    running = (peak_rows.T, total_rows.T, numerators)
    whole_cache = lax.all_gather(stale_cache, "patch", axis=1, tiled=True)
    key_count = whole_cache.shape[1]
    block_rows = block_length(key_count)
    stacked = whole_cache.reshape(2, key_count, whole_cache.shape[2] // HEAD_DIM, HEAD_DIM)

    def block_step(block_index, state):
        block_start = block_index * block_rows
        key_block = lax.dynamic_slice_in_dim(stacked[0], block_start, block_rows, 0)
        value_block = lax.dynamic_slice_in_dim(stacked[1], block_start, block_rows, 0)
        return update(state, key_block, value_block, 0 + block_start)

    running = lax.fori_loop(0, key_count // block_rows, block_step, running)
    peak_value, totals, numerators_now = running
    head_output = (numerators_now / totals.T[:, :, None]).astype(jnp.bfloat16)
    returned = lax.all_to_all(
        head_output.reshape(patch_rows, 1, heads_here, HEAD_DIM),
        "uly",
        split_axis=0,
        concat_axis=1,
        tiled=True,
    )
    attended = returned.reshape(tok_rows, width)
    fresh_cache = jnp.stack([key_heads, value_heads]).reshape(2, patch_rows, heads_here * HEAD_DIM)
    return (attended, fresh_cache)


def solution(mesh):
    in_specs = (
        P(("patch", "uly"), None),
        P(("patch", "uly"), None),
        P(("patch", "uly"), None),
        P(None, "patch", "uly"),
    )
    out_specs = (P(("patch", "uly"), None), P(None, "patch", "uly"))
    return jax.shard_map(local, mesh=mesh, in_specs=in_specs, out_specs=out_specs, check_vma=False)
```

profile of v0, /device:TPU:6, one launch (start us, length us, event | category | flops | bytes accessed | tf_op | source)
XLA Modules:
  0.0 220.2 jit_solution(1785649336785635700)
XLA Ops:
  7.2 0.0 all-gather.2.cloned.1.call-start
  7.2 1.9 copy.38
  9.1 0.0 all-gather.2.cloned.1.call-update
  9.1 1.2 reshape.52
  10.4 0.8 copy.31
  11.2 9.0 %all-to-all-start = ((bf16[16,16,3,128]{3,0,2,1:T(8,128)(2,1)}), bf16[16,16,3,128]{3,0,2,1:T(8,128)(2,1)S(1)}, u32[]{:S(2)}, u32[]{:S(2)}) async-start(bf16[16,16,3,128]{3,0,2,1:T(8,128)(2,1)} %copy.31), calls=%async_computation | async-start | bytes 393216 | tf_op jit(solution)/shard_map/all_to_all | solution.py:45
  20.2 1.2 reshape.53
  21.5 0.8 copy.33
  22.3 7.0 %all-to-all-done = bf16[16,16,3,128]{3,0,2,1:T(8,128)(2,1)S(1)} async-done(((bf16[16,16,3,128]{3,0,2,1:T(8,128)(2,1)}), bf16[16,16,3,128]{3,0,2,1:T(8,128)(2,1)S(1)}, u32[]{:S(2)}, u32[]{:S(2)}) %all-to-all-start) | async-done | bytes 196640 | tf_op jit(solution)/shard_map/all_to_all | solution.py:45
  29.3 4.2 %all-to-all-start.1 = ((bf16[16,16,3,128]{3,0,2,1:T(8,128)(2,1)}), bf16[16,16,3,128]{3,0,2,1:T(8,128)(2,1)S(1)}, u32[]{:S(2)}, u32[]{:S(2)}) async-start(bf16[16,16,3,128]{3,0,2,1:T(8,128)(2,1)} %copy.33), calls=%async_computation.1 | async-start | bytes 393216 | tf_op jit(solution)/shard_map/all_to_all | solution.py:46
  33.5 1.2 reshape.54
  34.7 0.8 copy.35
  35.5 6.9 %all-to-all-done.1 = bf16[16,16,3,128]{3,0,2,1:T(8,128)(2,1)S(1)} async-done(((bf16[16,16,3,128]{3,0,2,1:T(8,128)(2,1)}), bf16[16,16,3,128]{3,0,2,1:T(8,128)(2,1)S(1)}, u32[]{:S(2)}, u32[]{:S(2)}) %all-to-all-start.1) | async-done | bytes 196640 | tf_op jit(solution)/shard_map/all_to_all | solution.py:46
  42.5 3.9 %all-to-all-start.2 = ((bf16[16,16,3,128]{3,0,2,1:T(8,128)(2,1)}), bf16[16,16,3,128]{3,0,2,1:T(8,128)(2,1)S(1)}, u32[]{:S(2)}, u32[]{:S(2)}) async-start(bf16[16,16,3,128]{3,0,2,1:T(8,128)(2,1)} %copy.35), calls=%async_computation.2 | async-start | bytes 393216 | tf_op jit(solution)/shard_map/all_to_all | solution.py:47
  46.4 8.8 %all-to-all-done.2 = bf16[16,16,3,128]{3,0,2,1:T(8,128)(2,1)S(1)} async-done(((bf16[16,16,3,128]{3,0,2,1:T(8,128)(2,1)}), bf16[16,16,3,128]{3,0,2,1:T(8,128)(2,1)S(1)}, u32[]{:S(2)}, u32[]{:S(2)}) %all-to-all-start.2) | async-done | bytes 196640 | tf_op jit(solution)/shard_map/all_to_all | solution.py:47
  55.2 0.3 fusion.35
  55.5 0.3 convolution_bitcast_fusion
  55.8 0.2 copy.39
  56.0 0.1 fusion.30
  56.1 77.2 %all-gather.2.cloned.1.call-done = bf16[2,8192,384]{1,2,0:T(8,128)(2,1)} async-done(((bf16[2,256,384]{1,2,0:T(8,128)(2,1)}), bf16[2,8192,384]{1,2,0:T(8,128)(2,1)}) %all-gather.2.cloned.1.call-update) | async-done | bytes 12582928 | tf_op jit(solution)/shard_map/all_gather | solution.py:79
  133.3 16.6 %copy.40 = bf16[2,8192,3,128]{3,1,2,0:T(8,128)(2,1)} copy(bf16[2,8192,3,128]{1,3,2,0:T(8,128)(2,1)} %bitcast.82) | data formatting | bytes 25165824 | tf_op jit(solution)/shard_map/while | solution.py:90
  150.0 43.5 %while.18 = (s32[]{:T(128)}, f32[3,256]{1,0:T(4,128)S(1)}, f32[3,256]{1,0:T(4,128)S(1)}, f32[256,3,128]{0,2,1:T(8,128)S(1)}, s32[]{:T(128)}, /*index=5*/s32[]{:T...) while((s32[]{:T(128)}, f32[3,256]{1,0:T(4,128)S(1)}, ...), condition=%wide.region_5.6_spmd, body=%wide.region_2.5_spmd.sunk | while | flops 822814976 | bytes 48228532 | solution.py:90
  150.0 5.2 %fusion.52 = (bf16[1,8192,3,128]{3,1,2,0:T(8,128)(2,1)S(1)}, bf16[1,8192,3,128]{3,1,2,0:T(8,128)(2,1)S(1)}) fusion(bf16[2,8192,3,128]{3,1,2,0:T(8,128)(2,1)} %get-tuple-element.301), kind=kLoop, calls=%fused_computation.35.clone.1 | loop fusion | bytes 25165824 | tf_op jit(solution)/shard_map/while/body/eval_jaxpr/slice | solution.py:87
  155.2 2.0 bitcast_reduce_fusion.2
  157.3 2.1 fusion.55
  159.3 1.4 fusion.54
  160.8 5.2 %fusion.52 = (bf16[1,8192,3,128]{3,1,2,0:T(8,128)(2,1)S(1)}, bf16[1,8192,3,128]{3,1,2,0:T(8,128)(2,1)S(1)}) fusion(bf16[2,8192,3,128]{3,1,2,0:T(8,128)(2,1)} %get-tuple-element.301), kind=kLoop, calls=%fused_computation.35.clone.1 | loop fusion | bytes 25165824 | tf_op jit(solution)/shard_map/while/body/eval_jaxpr/slice | solution.py:87
  166.1 2.0 bitcast_reduce_fusion.2
  168.1 2.1 fusion.55
  170.2 1.4 fusion.54
  171.7 5.2 %fusion.52 = (bf16[1,8192,3,128]{3,1,2,0:T(8,128)(2,1)S(1)}, bf16[1,8192,3,128]{3,1,2,0:T(8,128)(2,1)S(1)}) fusion(bf16[2,8192,3,128]{3,1,2,0:T(8,128)(2,1)} %get-tuple-element.301), kind=kLoop, calls=%fused_computation.35.clone.1 | loop fusion | bytes 25165824 | tf_op jit(solution)/shard_map/while/body/eval_jaxpr/slice | solution.py:87
  177.0 2.0 bitcast_reduce_fusion.2
  179.0 2.1 fusion.55
  181.1 1.4 fusion.54
  182.6 5.2 %fusion.52 = (bf16[1,8192,3,128]{3,1,2,0:T(8,128)(2,1)S(1)}, bf16[1,8192,3,128]{3,1,2,0:T(8,128)(2,1)S(1)}) fusion(bf16[2,8192,3,128]{3,1,2,0:T(8,128)(2,1)} %get-tuple-element.301), kind=kLoop, calls=%fused_computation.35.clone.1 | loop fusion | bytes 25165824 | tf_op jit(solution)/shard_map/while/body/eval_jaxpr/slice | solution.py:87
  187.8 2.0 bitcast_reduce_fusion.2
  189.9 2.1 fusion.55
  191.9 1.4 fusion.54
  193.4 0.1 copy.41
  193.6 0.2 copy.42
  193.8 1.0 fusion.33
  194.9 6.9 %all-to-all-start.3 = ((bf16[256,1,3,128]{3,2,1,0:T(4,128)(2,1)}), bf16[256,1,3,128]{3,2,1,0:T(4,128)(2,1)S(1)}, u32[]{:S(2)}, u32[]{:S(2)}) async-start(bf16[256,1,3,128]{3,2,1,0:T(4,128)(2,1)} %fusion.33), calls=%async_computation.3 | async-start | bytes 524288 | tf_op jit(solution)/shard_map/all_to_all | solution.py:93
  201.8 0.1 copy.45
  201.9 0.1 copy.46
  202.0 0.2 stack.7
  202.2 0.2 stack.8
  202.4 0.8 pad_maximum_fusion
  203.2 9.2 %all-to-all-done.3 = bf16[256,1,3,128]{3,2,1,0:T(4,128)(2,1)S(1)} async-done(((bf16[256,1,3,128]{3,2,1,0:T(4,128)(2,1)}), bf16[256,1,3,128]{3,2,1,0:T(4,128)(2,1)S(1)}, u32[]{:S(2)}, u32[]{:S(2)}) %all-to-all-start.3) | async-done | bytes 196640 | tf_op jit(solution)/shard_map/all_to_all | solution.py:93
  212.4 0.2 copy.44
  212.5 0.9 reshape.57
  (20 shorter events, 0.2 us)
Async XLA Ops:
  7.2 126.2 %all-gather.2.cloned.1.call-start = ((), (), s32[]{:S(2)}) async-start(), calls=%async_computation.4 | async-start | bytes 12976128 | tf_op jit(solution)/shard_map/all_gather | solution.py:79
  11.2 18.1 %all-to-all-start = ((bf16[16,16,3,128]{3,0,2,1:T(8,128)(2,1)}), bf16[16,16,3,128]{3,0,2,1:T(8,128)(2,1)S(1)}, u32[]{:S(2)}, u32[]{:S(2)}) async-start(bf16[16,16,3,128]{3,0,2,1:T(8,128)(2,1)} %copy.31), calls=%async_computation | async-start | bytes 393216 | tf_op jit(solution)/shard_map/all_to_all | solution.py:45
  29.3 13.2 %all-to-all-start.1 = ((bf16[16,16,3,128]{3,0,2,1:T(8,128)(2,1)}), bf16[16,16,3,128]{3,0,2,1:T(8,128)(2,1)S(1)}, u32[]{:S(2)}, u32[]{:S(2)}) async-start(bf16[16,16,3,128]{3,0,2,1:T(8,128)(2,1)} %copy.33), calls=%async_computation.1 | async-start | bytes 393216 | tf_op jit(solution)/shard_map/all_to_all | solution.py:46
  42.5 12.7 %all-to-all-start.2 = ((bf16[16,16,3,128]{3,0,2,1:T(8,128)(2,1)}), bf16[16,16,3,128]{3,0,2,1:T(8,128)(2,1)S(1)}, u32[]{:S(2)}, u32[]{:S(2)}) async-start(bf16[16,16,3,128]{3,0,2,1:T(8,128)(2,1)} %copy.35), calls=%async_computation.2 | async-start | bytes 393216 | tf_op jit(solution)/shard_map/all_to_all | solution.py:47
  194.9 17.5 %all-to-all-start.3 = ((bf16[256,1,3,128]{3,2,1,0:T(4,128)(2,1)}), bf16[256,1,3,128]{3,2,1,0:T(4,128)(2,1)S(1)}, u32[]{:S(2)}, u32[]{:S(2)}) async-start(bf16[256,1,3,128]{3,2,1,0:T(4,128)(2,1)} %fusion.33), calls=%async_computation.3 | async-start | bytes 524288 | tf_op jit(solution)/shard_map/all_to_all | solution.py:93
Sparse Core Ops, SparseCore 0:
  11.6 121.6 all-gather.1
where the time goes:
time: 222 us; the launch traced here: 220 us
  waiting for transfers between devices  109 us (49%)
  local copies, waits for them, and re-layouts  47.9 us (22%)
  starting transfers between devices  24 us (11%)
  matrix products  16.9 us (8%)
  between operations  14.2 us (6%)
  other arithmetic  7.9 us (4%)
    all_gather x1, waiting for transfers between devices, local(): whole_cache = lax.all_gather(stale_cache, 'patch', axis=1, tiled=True)  77.2 us
    slice x4, local copies, waits for them, and re-layouts, block_step(): stacked[1]  20.9 us
    while x3, local copies, waits for them, and re-layouts, local(): running = lax.fori_loop(0, key_count // block_rows, block_step, running)  17 us
    all_to_all x1, waiting for transfers between devices, local(): lax.all_to_all(head_output.reshape(patch_rows, 1, heads_here, HEAD_DIM),...  9.16 us
    all_to_all x1, starting transfers between devices, local(): lax.all_to_all(by_group(queries), 'uly', split_axis=1, concat_axis=0, til...  9.01 us
    all_to_all x1, waiting for transfers between devices, local(): lax.all_to_all(by_group(values), 'uly', split_axis=1, concat_axis=0, tile...  8.82 us
    dot_general x4, matrix products, update(): jnp.einsum('hqk,khd->qhd', weights.astype(jnp.bfloat16), value_block, pre...  8.26 us
    dot_general x4, matrix products, update(): jnp.einsum('qhd,khd->hqk', query_heads, key_block, preferred_element_type...  8.07 us
  transfers between devices with their start and end apart: 5, of which 5 were waited for; matrix products, arithmetic and copies ran while one was open for 4% of the time, Pallas kernels for 0%

commit v1 on v0

v1 whole, which is shorter than its diff:
```python
import jax
import jax.numpy as jnp
from jax import lax
from jax.experimental import pallas as pl
from jax.experimental.pallas import tpu as pltpu
from jax.sharding import PartitionSpec as P

MESH = pl.DeviceIdType.MESH
HEADS = 48
HD = 128
SCALE = 1.4426950408889634 * HD**-0.5

KINDS = (
    [(t, r) for t in "KV" for r in ("z", "x", "s0", "xz", "s1", "s2", "s3")]
    + [("Q", r) for r in ("z", "x", "xz")]
    + [(t, r) for t in "OT" for r in (0, 1, 2)]
)
KIND_INDEX = {kind: i for i, kind in enumerate(KINDS)}


def kernel(
    q_hbm, k_hbm, v_hbm, stale, out, fresh,
    ka, va, qa, qland, kland, vland, stale_v,
    scores, part_o, part_t, send_o, send_t, got_o, got_t, final,
    ssem, rsem, a2a_s, a2a_r, ao_s, ao_r, lsem,
):
    rows, width = q_hbm.shape
    uly = width // qland.shape[1]
    nh = qland.shape[1] // HD
    patch = lax.axis_index("patch")
    me = lax.axis_index("uly")
    core = patch % 2
    x = (patch // 2) % 4
    zh = patch // 8

    def at_patch(zh_, x_, core_):
        return ((zh_ * 4 + x_) * 2 + core_, me)

    sib = at_patch(zh, x, 1 - core)
    zk = at_patch(zh + 1 - 2 * (zh % 2), x, core)
    xk = at_patch(zh, x + 1 - 2 * (x % 2), core)
    zq = at_patch(3 - zh, x, core)
    xq = at_patch(zh, 3 - x, core)

    def copy(kind, h):
        t, r = kind
        if t in "KV":
            slots = ka if t == "K" else va
            own = slots.at[0, h]
            src, dst, to = {
                "z": (own, 1, zk),
                "x": (own, 2, xk),
                "s0": (own, 4, sib),
                "xz": (slots.at[1, h], 3, xk),
                "s1": (slots.at[1, h], 5, sib),
                "s2": (slots.at[2, h], 6, sib),
                "s3": (slots.at[3, h], 7, sib),
            }[r]
            dst = slots.at[dst, h]
        elif t == "Q":
            src, dst, to = {"z": (3, 2, zq), "x": (3, 1, xq), "xz": (2, 0, xq)}[r]
            src, dst = qa.at[src, h], qa.at[dst, h]
        else:
            src = (send_o if t == "O" else send_t).at[h, r]
            dst = (got_o if t == "O" else got_t).at[h, r]
            to = zq if r == 2 else xq
        i = KIND_INDEX[kind] * nh + h
        return pltpu.make_async_remote_copy(
            src_ref=src, dst_ref=dst, send_sem=ssem.at[i], recv_sem=rsem.at[i],
            device_id=to, device_id_type=MESH,
        )

    def start(t, r, h):
        copy((t, r), h).start()

    def arrived(t, r, h):
        copy((t, r), h).wait_recv()

    cut = pl.ds(pl.multiple_of(me * nh * HD, HD), nh * HD)
    mine = pl.ds(pl.multiple_of(me * rows, rows), rows)
    local = [pltpu.make_async_copy(stale.at[1], stale_v, lsem.at[0])]
    for i, (src, dst) in enumerate(((q_hbm, qland), (k_hbm, kland), (v_hbm, vland))):
        local.append(pltpu.make_async_copy(src.at[:, cut], dst.at[mine], lsem.at[1 + i]))
    for h in range(nh):
        local.append(
            pltpu.make_async_copy(stale.at[0, :, pl.ds(h * HD, HD)], ka.at[0, h], lsem.at[4 + h])
        )
    for c in local:
        c.start()

    barrier = pltpu.get_barrier_semaphore()
    for i in range(1, uly):
        pl.semaphore_signal(
            barrier, inc=1, device_id=(patch, (me + i) % uly), device_id_type=MESH
        )
    for to in (sib, zk, xk, zq, xq):
        pl.semaphore_signal(barrier, inc=1, device_id=to, device_id_type=MESH)

    local[0].wait()
    for h in range(nh):
        va[0, h] = stale_v[:, h * HD : (h + 1) * HD].T
    for h in range(nh):
        local[4 + h].wait()
    pl.semaphore_wait(barrier, uly - 1 + 5)

    def exchange(n, src, dst):
        for i in range(1, uly):
            peer = (me + i) % uly
            pltpu.make_async_remote_copy(
                src_ref=src.at[:, pl.ds(pl.multiple_of(peer * nh * HD, HD), nh * HD)],
                dst_ref=dst.at[mine],
                send_sem=a2a_s.at[n], recv_sem=a2a_r.at[n],
                device_id=(patch, peer), device_id_type=MESH,
            ).start()

    def exchanged(n, dst):
        whole = dst.at[pl.ds(0, (uly - 1) * rows)]
        pltpu.make_async_copy(whole, whole, a2a_r.at[n]).wait()
        local[1 + n].wait()

    exchange(0, q_hbm, qland)
    for h in range(nh):
        for t in "KV":
            start(t, "z", h)
            start(t, "x", h)
            start(t, "s0", h)
    exchange(1, k_hbm, kland)
    exchange(2, v_hbm, vland)
    exchanged(0, qland)
    for h in range(nh):
        qa[3, h] = qland[:, h * HD : (h + 1) * HD]
        start("Q", "z", h)
        start("Q", "x", h)

    def forward_z(t, h):
        arrived(t, "z", h)
        start(t, "xz", h)
        start(t, "s1", h)

    def forward_x(h):
        arrived("Q", "z", h)
        start("Q", "xz", h)
        for t in "KV":
            arrived(t, "x", h)
            start(t, "s2", h)

    def forward_xz(h):
        for t in "KV":
            arrived(t, "xz", h)
            start(t, "s3", h)

    def ready(h):
        for t in "KV":
            for r in ("s0", "s1", "s2", "s3"):
                arrived(t, r, h)
        arrived("Q", "x", h)
        arrived("Q", "xz", h)

    def take_fresh():
        exchanged(1, kland)
        exchanged(2, vland)
        pltpu.make_async_copy(kland, fresh.at[0], lsem.at[7]).start()
        pltpu.make_async_copy(vland, fresh.at[1], lsem.at[8]).start()
        for h in range(nh):
            ka[8, h] = kland[:, h * HD : (h + 1) * HD]
            va[8, h] = vland[:, h * HD : (h + 1) * HD].T

    def stats(m, l):
        row = lax.broadcasted_iota(jnp.int32, (8, m.shape[1]), 0)
        return jnp.where(row < 4, jnp.broadcast_to(m, row.shape), jnp.broadcast_to(l, row.shape))

    def combine(o1, t1, o2, t2):
        m1, l1, m2, l2 = t1[0:1], t1[4:5], t2[0:1], t2[4:5]
        m = jnp.maximum(m1, m2)
        a1 = l1 * jnp.exp2((m1 - m) * SCALE)
        a2 = l2 * jnp.exp2((m2 - m) * SCALE)
        l = a1 + a2
        return o1 * (a1 / l) + o2.astype(jnp.float32) * (a2 / l), stats(m, l)

    def combine_x(h):
        arrived("O", 0, h)
        arrived("T", 0, h)
        o, t = combine(part_o[h, 0], part_t[h, 0], got_o[h, 0], got_t[h, 0])
        send_o[h, 2] = o.astype(jnp.bfloat16)
        send_t[h, 2] = t
        start("O", 2, h)
        start("T", 2, h)
        arrived("O", 1, h)
        arrived("T", 1, h)
        o, t = combine(part_o[h, 1], part_t[h, 1], got_o[h, 1], got_t[h, 1])
        part_o[h, 1] = o
        part_t[h, 1] = t

    def out_columns(h):
        return pl.ds(pl.multiple_of((me * nh + h) * HD, HD), HD)

    def combine_z(h):
        arrived("O", 2, h)
        arrived("T", 2, h)
        o, _ = combine(part_o[h, 1], part_t[h, 1], got_o[h, 2], got_t[h, 2])
        final[h] = o.T.astype(jnp.bfloat16)
        pltpu.make_async_copy(final.at[h, mine], out.at[:, out_columns(h)], lsem.at[9 + h]).start()
        for i in range(1, uly):
            peer = (me + i) % uly
            pltpu.make_async_remote_copy(
                src_ref=final.at[h, pl.ds(pl.multiple_of(peer * rows, rows), rows)],
                dst_ref=out.at[:, out_columns(h)],
                send_sem=ao_s.at[h], recv_sem=ao_r.at[h],
                device_id=(patch, peer), device_id_type=MESH,
            ).start()

    def prepare(h):
        forward_z("K", h)
        forward_z("V", h)
        forward_x(h)
        forward_xz(h)
        ready(h)

    plan = {
        0: lambda: prepare(0),
        1: lambda: forward_z("K", 1),
        2: lambda: (forward_z("V", 1), forward_x(1)),
        3: take_fresh,
        4: lambda: (forward_xz(1), ready(1)),
        5: lambda: (forward_z("K", 2), combine_x(0)),
        6: lambda: (forward_z("V", 2), forward_x(2)),
        7: lambda: combine_z(0),
        8: lambda: (forward_xz(2), ready(2)),
        9: lambda: combine_x(1),
        11: lambda: combine_z(1),
    }
    blk = ka.shape[2]

    def attend(h, j):
        q = qa[j, h]
        first = (j // 3) * 8
        m8 = None
        for b in range(8):
            k = ka[first if b == 0 else b, h]
            s = lax.dot_general(k, q, (((1,), (1,)), ((), ())), preferred_element_type=jnp.float32)
            scores[b * blk : (b + 1) * blk] = s
            top = jnp.max(s.reshape(blk // 8, 8, s.shape[1]), axis=0)
            m8 = top if m8 is None else jnp.maximum(m8, top)
        m = jnp.max(m8, axis=0, keepdims=True)
        l8 = jnp.zeros_like(m8)
        acc = jnp.zeros((HD, q.shape[0]), jnp.float32)
        for b in range(8):
            w = jnp.exp2((scores[b * blk : (b + 1) * blk] - m) * SCALE)
            l8 = l8 + jnp.sum(w.reshape(blk // 8, 8, w.shape[1]), axis=0)
            acc = acc + jnp.dot(
                va[first if b == 0 else b, h], w.astype(jnp.bfloat16),
                preferred_element_type=jnp.float32,
            )
        l = jnp.sum(l8, axis=0, keepdims=True)
        return acc * (1.0 / l), stats(m, l)

    def step(s, _):
        for at, action in plan.items():
            pl.when(s == at)(lambda action=action: (action(), None)[1])
        h, j = s // 4, s % 4
        o, t = attend(h, j)

        @pl.when(j < 2)
        def _():
            send_o[h, j] = o.astype(jnp.bfloat16)
            send_t[h, j] = t

        for r in (0, 1):

            @pl.when(j == r)
            def _(r=r):
                start("O", r, h)
                start("T", r, h)

        @pl.when(j >= 2)
        def _():
            part_o[h, j - 2] = o
            part_t[h, j - 2] = t

        return 0

    lax.fori_loop(0, 4 * nh, step, 0)
    combine_x(nh - 1)
    combine_z(nh - 1)

    for h in range(nh):
        some = out.at[:, pl.ds(0, (uly - 1) * HD)]
        pltpu.make_async_copy(some, some, ao_r.at[h]).wait()
        pltpu.make_async_copy(some, some, ao_s.at[h]).wait()
        pltpu.make_async_copy(final.at[h, mine], out.at[:, out_columns(h)], lsem.at[9 + h]).wait()
    for n, dst in enumerate((qland, kland, vland)):
        whole = dst.at[pl.ds(0, (uly - 1) * rows)]
        pltpu.make_async_copy(whole, whole, a2a_s.at[n]).wait()
    pltpu.make_async_copy(kland, fresh.at[0], lsem.at[7]).wait()
    pltpu.make_async_copy(vland, fresh.at[1], lsem.at[8]).wait()
    for kind in KINDS:
        for h in range(nh):
            copy(kind, h).wait_send()


def local(queries, keys, values, stale_cache):
    rows, width = queries.shape
    _, patch_rows, cols = stale_cache.shape
    nh = cols // HD
    bf, f32 = jnp.bfloat16, jnp.float32
    n_copies = len(KINDS) * nh
    vm = pltpu.VMEM
    dma = pltpu.SemaphoreType.DMA
    return pl.pallas_call(
        kernel,
        out_shape=(
            jax.ShapeDtypeStruct((rows, width), bf),
            jax.ShapeDtypeStruct(stale_cache.shape, bf),
        ),
        in_specs=[pl.BlockSpec(memory_space=pl.ANY)] * 4,
        out_specs=(pl.BlockSpec(memory_space=pl.ANY),) * 2,
        scratch_shapes=[
            vm((9, nh, patch_rows, HD), bf),
            vm((9, nh, HD, patch_rows), bf),
            vm((4, nh, patch_rows, HD), bf),
            vm((patch_rows, cols), bf),
            vm((patch_rows, cols), bf),
            vm((patch_rows, cols), bf),
            vm((patch_rows, cols), bf),
            vm((8 * patch_rows, patch_rows), f32),
            vm((nh, 2, HD, patch_rows), f32),
            vm((nh, 2, 8, patch_rows), f32),
            vm((nh, 3, HD, patch_rows), bf),
            vm((nh, 3, 8, patch_rows), f32),
            vm((nh, 3, HD, patch_rows), bf),
            vm((nh, 3, 8, patch_rows), f32),
            vm((nh, patch_rows, HD), bf),
            dma((n_copies,)),
            dma((n_copies,)),
            dma((3,)),
            dma((3,)),
            dma((nh,)),
            dma((nh,)),
            dma((9 + nh,)),
        ],
        compiler_params=pltpu.CompilerParams(
            collective_id=0, has_side_effects=True, vmem_limit_bytes=40 * 2**20
        ),
        cost_estimate=pl.CostEstimate(
            flops=4 * 8 * 4 * patch_rows**2 * cols,
            bytes_accessed=8 * patch_rows * cols,
            transcendentals=32 * patch_rows**2 * nh,
        ),
    )(queries, keys, values, stale_cache)


def solution(mesh):
    in_specs = (
        P(("patch", "uly"), None),
        P(("patch", "uly"), None),
        P(("patch", "uly"), None),
        P(None, "patch", "uly"),
    )
    out_specs = (P(("patch", "uly"), None), P(None, "patch", "uly"))
    return jax.shard_map(local, mesh=mesh, in_specs=in_specs, out_specs=out_specs, check_vma=False)
```

time: 222 us -> 81.1 us (0.37)
  waiting for transfers between devices: 109 us -> 0 us
  Pallas kernels: 0 us -> 74 us
  local copies, waits for them, and re-layouts: 47.9 us -> 5.19 us
  starting transfers between devices: 24 us -> 0 us
  matrix products: 16.9 us -> 0 us
  between operations: 14.2 us -> 0.65 us
  other arithmetic: 7.9 us -> 0 us
    all_gather x1 -> x0, waiting for transfers between devices: 77.2 us -> none  [local(): whole_cache = lax.all_gather(stale_cache, 'patch', axis=1, tiled=True)]
    pallas_call x0 -> x1, Pallas kernels: none -> 74 us  [local(): pl.pallas_call(kernel, out_shape=(jax.ShapeDtypeStruct((rows, width), bf)...]
    all_to_all x4 -> x0, waiting for transfers between devices: 31.9 us -> none  [the longest x1 9.16 us: local(): lax.all_to_all(head_output.reshape(patch_rows, 1, heads_here, HEAD_DIM),...]
    all_to_all x4 -> x0, starting transfers between devices: 24 us -> none  [the longest x1 9.01 us: local(): lax.all_to_all(by_group(queries), 'uly', split_axis=1, concat_axis=0, til...]
    slice x4 -> x0, local copies, waits for them, and re-layouts: 20.9 us -> none  [block_step(): stacked[1]]
    while x7 -> x0, local copies, waits for them, and re-layouts: 17 us -> none  [the longest x3 17 us: local(): running = lax.fori_loop(0, key_count // block_rows, block_step, running)]
    dot_general x10 -> x0, matrix products: 16.9 us -> none  [the longest x4 8.26 us: update(): jnp.einsum('hqk,khd->qhd', weights.astype(jnp.bfloat16), value_block, pre...]
    reshape x7 -> x0, local copies, waits for them, and re-layouts: 7.03 us -> none  [the longest x6 6.18 us: by_group(): return matrix.reshape(tok_rows, uly_count, heads_here, HEAD_DIM)]
  transfers between devices with their start and end apart: 5 -> 0, of which waited for: 5 -> 0; matrix products, arithmetic and copies ran while one was open for 4% -> 0% of each run, Pallas kernels for 0% -> 0%
where the time goes in v1:
time: 81.1 us; the launch traced here: 79.8 us
  Pallas kernels  74 us (91%)
  local copies, waits for them, and re-layouts  5.19 us (6%)
    pallas_call x1, Pallas kernels, local(): pl.pallas_call(kernel, out_shape=(jax.ShapeDtypeStruct((rows, width), bf)...  74 us
    unnamed x10, local copies, waits for them, and re-layouts  5.19 us

profile of v1, /device:TPU:6, one launch (start us, length us, event | category | flops | bytes accessed | tf_op | source)
XLA Modules:
  0.0 79.8 jit_solution(1963595133974922484)
XLA Ops:
  0.6 0.0 copy-start
  0.6 1.0 %copy-done = bf16[2,256,384]{2,1,0:T(8,128)(2,1)S(1)} copy-done((bf16[2,256,384]{2,1,0:T(8,128)(2,1)S(1)}, bf16[2,256,384]{2,1,0:T(8,128)(2,1)}, u32[]{:S(2)}) %copy-start) | copy-done | bytes 393240
  1.6 0.0 copy-start.1
  1.6 0.9 %copy-done.1 = bf16[16,6144]{1,0:T(8,128)(2,1)S(1)} copy-done((bf16[16,6144]{1,0:T(8,128)(2,1)S(1)}, bf16[16,6144]{1,0:T(8,128)(2,1)}, u32[]{:S(2)}) %copy-start.1) | copy-done | bytes 196632
  2.6 0.0 copy-start.2
  2.6 0.9 %copy-done.2 = bf16[16,6144]{1,0:T(8,128)(2,1)S(1)} copy-done((bf16[16,6144]{1,0:T(8,128)(2,1)S(1)}, bf16[16,6144]{1,0:T(8,128)(2,1)}, u32[]{:S(2)}) %copy-start.2) | copy-done | bytes 196632
  3.5 0.0 copy-start.3
  3.5 0.9 %copy-done.3 = bf16[16,6144]{1,0:T(8,128)(2,1)S(1)} copy-done((bf16[16,6144]{1,0:T(8,128)(2,1)S(1)}, bf16[16,6144]{1,0:T(8,128)(2,1)}, u32[]{:S(2)}) %copy-start.3) | copy-done | bytes 196632
  4.4 74.0 %shard_map.59 = (bf16[16,6144]{1,0:T(8,128)(2,1)S(1)}, bf16[2,256,384]{2,1,0:T(8,128)(2,1)S(1)}) custom-call(bf16[16,6144]{1,0:T(8,128)(2,1)S(1)} %copy-done.1, bf16[16,6144]{1,0:T(8,128)(2,1)S(1)} %copy-done.2, bf16[16,6144]{1,0:T(8,128)(2,1)S(1)} %copy-done.3, bf16[2,256,384]{2,1,0:T(8,128)(2,1)S(1)} %copy-done), custom_call_target="tpu_custom_call" | custom-call | flops 3221225472 | bytes 786432 | tf_op jit(solution)/shard_map/pallas_call | solution.py:309
  78.4 0.7 copy.8
  79.1 0.7 copy.9
Async XLA Ops:
  0.6 1.0 %copy-start = (bf16[2,256,384]{2,1,0:T(8,128)(2,1)S(1)}, bf16[2,256,384]{2,1,0:T(8,128)(2,1)}, u32[]{:S(2)}) copy-start(bf16[2,256,384]{2,1,0:T(8,128)(2,1)} %stale.1) | copy-start | bytes 1179652
  1.6 0.9 %copy-start.1 = (bf16[16,6144]{1,0:T(8,128)(2,1)S(1)}, bf16[16,6144]{1,0:T(8,128)(2,1)}, u32[]{:S(2)}) copy-start(bf16[16,6144]{1,0:T(8,128)(2,1)} %q_hbm.1) | copy-start | bytes 589828
  2.6 0.9 %copy-start.2 = (bf16[16,6144]{1,0:T(8,128)(2,1)S(1)}, bf16[16,6144]{1,0:T(8,128)(2,1)}, u32[]{:S(2)}) copy-start(bf16[16,6144]{1,0:T(8,128)(2,1)} %k_hbm.1) | copy-start | bytes 589828
  3.5 0.9 %copy-start.3 = (bf16[16,6144]{1,0:T(8,128)(2,1)S(1)}, bf16[16,6144]{1,0:T(8,128)(2,1)}, u32[]{:S(2)}) copy-start(bf16[16,6144]{1,0:T(8,128)(2,1)} %v_hbm.1) | copy-start | bytes 589828

commit v2 on v1

v2 whole, which is shorter than its diff:
```python
import jax
import jax.numpy as jnp
from jax import lax
from jax.experimental import pallas as pl
from jax.experimental.pallas import tpu as pltpu
from jax.sharding import PartitionSpec as P

MESH = pl.DeviceIdType.MESH
HEADS = 48
HD = 128
SCALE = 1.4426950408889634 * HD**-0.5

KINDS = (
    [(t, r) for t in "KV" for r in ("z", "x", "s0", "xz", "s1", "s2", "s3")]
    + [("Q", r) for r in ("z", "x", "xz")]
    + [(t, r) for t in "OT" for r in (0, 1, 2)]
)
KIND_INDEX = {kind: i for i, kind in enumerate(KINDS)}


def kernel(
    q_hbm, k_hbm, v_hbm, stale, out, fresh,
    ka, va, qa, qland, kland, vland, stale_v,
    scores, part_o, part_t, send_o, send_t, got_o, got_t, final,
    ssem, rsem, a2a_s, a2a_r, ao_s, ao_r, lsem,
):
    rows, width = q_hbm.shape
    uly = width // qland.shape[1]
    nh = qland.shape[1] // HD
    patch = lax.axis_index("patch")
    me = lax.axis_index("uly")
    core = patch % 2
    x = (patch // 2) % 4
    zh = patch // 8

    def at_patch(zh_, x_, core_):
        return ((zh_ * 4 + x_) * 2 + core_, me)

    sib = at_patch(zh, x, 1 - core)

    def flip(i, crossed):
        return (i + 1 - 2 * (i % 2)) * (1 - crossed) + (3 - i) * crossed

    def partner(r, crossed):
        return at_patch(
            flip(zh, crossed) if "z" in r else zh, flip(x, crossed) if "x" in r else x, core
        )

    def copy(kind, h):
        t, r = kind
        if t in "KV":
            slots = ka if t == "K" else va
            src, dst, to = {
                "z": (0, 1, "z"),
                "x": (0, 2, "x"),
                "s0": (0, 4, ""),
                "xz": (1, 3, "x"),
                "s1": (1, 5, ""),
                "s2": (2, 6, ""),
                "s3": (3, 7, ""),
            }[r]
            if t == "K" and src == 0:
                src = stale.at[0, :, pl.ds(h * HD, HD)]
            else:
                src = slots.at[src, h]
            dst = slots.at[dst, h]
            to = partner(to, h % 2) if to else sib
        elif t == "Q":
            src, dst = qa.at[3, h], qa.at[("xz", "x", "z").index(r), h]
            to = partner(r, 1 - h % 2)
        else:
            src = (send_o if t == "O" else send_t).at[h, r]
            dst = (got_o if t == "O" else got_t).at[h, r]
            to = partner(("xz", "x", "z")[r], 1 - h % 2)
        i = KIND_INDEX[kind] * nh + h
        return pltpu.make_async_remote_copy(
            src_ref=src, dst_ref=dst, send_sem=ssem.at[i], recv_sem=rsem.at[i],
            device_id=to, device_id_type=MESH,
        )

    def start(t, r, h):
        copy((t, r), h).start()

    def arrived(t, r, h):
        copy((t, r), h).wait_recv()

    barrier = pltpu.get_barrier_semaphore()
    ring = uly // 2
    steps = [(dz, dy) for dz in range(2) for dy in range(ring) if dz + dy]
    steps.sort(key=lambda d: -d[0] - min(d[1], ring - d[1]))
    peers = [((me // ring + dz) % 2) * ring + (me + dy) % ring for dz, dy in steps]
    for peer in peers:
        pl.semaphore_signal(barrier, inc=1, device_id=(patch, peer), device_id_type=MESH)
    near = [sib] + [partner(r, crossed) for r in ("z", "x", "xz") for crossed in (0, 1)]
    for to in near:
        pl.semaphore_signal(barrier, inc=1, device_id=to, device_id_type=MESH)

    cut = pl.ds(pl.multiple_of(me * nh * HD, HD), nh * HD)
    mine = pl.ds(pl.multiple_of(me * rows, rows), rows)
    local = [pltpu.make_async_copy(stale.at[1], stale_v, lsem.at[0])]
    for i, (src, dst) in enumerate(((q_hbm, qland), (k_hbm, kland), (v_hbm, vland))):
        local.append(pltpu.make_async_copy(src.at[:, cut], dst.at[mine], lsem.at[1 + i]))
    for h in range(nh):
        local.append(
            pltpu.make_async_copy(stale.at[0, :, pl.ds(h * HD, HD)], ka.at[0, h], lsem.at[4 + h])
        )
    for c in local:
        c.start()

    pl.semaphore_wait(barrier, uly - 1 + len(near))

    def exchange(n, src, dst):
        for peer in peers:
            pltpu.make_async_remote_copy(
                src_ref=src.at[:, pl.ds(pl.multiple_of(peer * nh * HD, HD), nh * HD)],
                dst_ref=dst.at[mine],
                send_sem=a2a_s.at[n], recv_sem=a2a_r.at[n],
                device_id=(patch, peer), device_id_type=MESH,
            ).start()

    def exchanged(n, dst):
        whole = dst.at[pl.ds(0, (uly - 1) * rows)]
        pltpu.make_async_copy(whole, whole, a2a_r.at[n]).wait()
        local[1 + n].wait()

    def forward_z(t, h):
        arrived(t, "z", h)
        start(t, "xz", h)
        start(t, "s1", h)

    def forward_x(t, h):
        arrived(t, "x", h)
        start(t, "s2", h)

    def forward_xz(t, h):
        arrived(t, "xz", h)
        start(t, "s3", h)

    def ready(t, h):
        for r in ("s0", "s1", "s2", "s3"):
            arrived(t, r, h)

    def start_both(r, h):
        for t in "KV":
            start(t, r, h)

    def start_query(h):
        qa[3, h] = qland[:, h * HD : (h + 1) * HD]
        for r in ("xz", "z", "x"):
            start("Q", r, h)

    exchange(0, q_hbm, qland)
    for h in (0, 1):
        for r in ("z", "x", "s0"):
            start("K", r, h)
    local[0].wait()
    for h in range(nh):
        va[0, h] = stale_v[:, h * HD : (h + 1) * HD].T
        if h < 2:
            for r in ("z", "x", "s0"):
                start("V", r, h)
    for h in range(nh):
        local[4 + h].wait()
    for t in "KV":
        forward_z(t, 0)
    start_both("z", 2)
    for t in "KV":
        forward_z(t, 1)
    for h in (0, 1):
        for t in "KV":
            forward_x(t, h)
    exchanged(0, qland)
    start_query(0)
    start_query(1)
    start_query(2)
    exchange(1, k_hbm, kland)
    exchange(2, v_hbm, vland)
    for t in "KV":
        forward_xz(t, 0)
    start_both("x", 2)
    start_both("s0", 2)
    for t in "KV":
        forward_xz(t, 1)
    ready("K", 0)
    arrived("Q", "x", 0)

    def take_fresh():
        exchanged(1, kland)
        exchanged(2, vland)
        pltpu.make_async_copy(kland, fresh.at[0], lsem.at[7]).start()
        pltpu.make_async_copy(vland, fresh.at[1], lsem.at[8]).start()
        for h in range(nh):
            ka[8, h] = kland[:, h * HD : (h + 1) * HD]
            va[8, h] = vland[:, h * HD : (h + 1) * HD].T

    def stats(m, l):
        row = lax.broadcasted_iota(jnp.int32, (8, m.shape[1]), 0)
        return jnp.where(row < 4, jnp.broadcast_to(m, row.shape), jnp.broadcast_to(l, row.shape))

    def out_columns(h):
        return pl.ds(pl.multiple_of((me * nh + h) * HD, HD), HD)

    def finish(h):
        for r in range(3):
            arrived("O", r, h)
            arrived("T", r, h)
        ts = [part_t[h]] + [got_t[h, r] for r in range(3)]
        m = jnp.maximum(
            jnp.maximum(ts[0][0:1], ts[1][0:1]), jnp.maximum(ts[2][0:1], ts[3][0:1])
        )
        shares = [t[4:5] * jnp.exp2((t[0:1] - m) * SCALE) for t in ts]
        inverse = 1.0 / (shares[0] + shares[1] + shares[2] + shares[3])
        o = part_o[h] * (shares[0] * inverse)
        for r in range(3):
            o = o + got_o[h, r].astype(jnp.float32) * (shares[1 + r] * inverse)
        final[h] = o.T.astype(jnp.bfloat16)
        pltpu.make_async_copy(final.at[h, mine], out.at[:, out_columns(h)], lsem.at[9 + h]).start()
        for peer in peers:
            pltpu.make_async_remote_copy(
                src_ref=final.at[h, pl.ds(pl.multiple_of(peer * rows, rows), rows)],
                dst_ref=out.at[:, out_columns(h)],
                send_sem=ao_s.at[h], recv_sem=ao_r.at[h],
                device_id=(patch, peer), device_id_type=MESH,
            ).start()

    order = (
        (0, 1), (0, 2), (0, 0), (1, 1), (1, 2), (1, 0),
        (0, 3), (2, 2), (2, 0), (1, 3), (2, 1), (2, 3),
    )
    plan = {
        0: lambda: (ready("V", 0), arrived("Q", "z", 0)),
        1: lambda: ([forward_z(t, 2) for t in "KV"], arrived("Q", "xz", 0)),
        2: lambda: (ready("K", 1), arrived("Q", "x", 1)),
        3: lambda: (
            ready("V", 1),
            [forward_x(t, 2) for t in "KV"],
            [forward_xz(t, 2) for t in "KV"],
            arrived("Q", "z", 1),
        ),
        4: lambda: arrived("Q", "xz", 1),
        5: take_fresh,
        6: lambda: (ready("K", 2), arrived("Q", "z", 2)),
        7: lambda: (ready("V", 2), arrived("Q", "xz", 2)),
        8: lambda: finish(0),
        9: lambda: arrived("Q", "x", 2),
        10: lambda: finish(1),
    }
    blk = ka.shape[2]

    def pick(s, values):
        r = values[0]
        for i, v in enumerate(values):
            r = jnp.where(s == i, v, r)
        return r

    def item(s):
        return pick(s, [h for h, _ in order]), pick(s, [j for _, j in order])

    def score(h, j, slot, b):
        k = ka[(j // 3) * 8 if b == 0 else b, h]
        s = lax.dot_general(
            k, qa[j, h], (((1,), (1,)), ((), ())), preferred_element_type=jnp.float32
        )
        scores[slot, b * blk : (b + 1) * blk] = s
        return jnp.max(s.reshape(blk // 8, 8, s.shape[1]), axis=0)

    def gather_values(h, j, slot, b, m):
        w = jnp.exp2((scores[slot, b * blk : (b + 1) * blk] - m) * SCALE)
        o = jnp.dot(
            va[(j // 3) * 8 if b == 0 else b, h], w.astype(jnp.bfloat16),
            preferred_element_type=jnp.float32,
        )
        return o, jnp.sum(w.reshape(blk // 8, 8, w.shape[1]), axis=0)

    def attend(now, later, slot, m8):
        m = jnp.max(m8, axis=0, keepdims=True)
        o, l8, new = 0.0, 0.0, None
        for b in range(8):
            o_b, l_b = gather_values(*now, slot, b, m)
            o, l8 = o + o_b, l8 + l_b
            if later is not None:
                top = score(*later, 1 - slot, b)
                new = top if new is None else jnp.maximum(new, top)
        l = jnp.sum(l8, axis=0, keepdims=True)
        return o * (1.0 / l), stats(m, l), new

    m8 = None
    for b in range(8):
        top = score(*order[0], 0, b)
        m8 = top if m8 is None else jnp.maximum(m8, top)

    def step(s, m8):
        for at, action in plan.items():
            pl.when(s == at)(lambda action=action: (action(), None)[1])
        h, j = item(s)
        o, t, m8 = attend((h, j), item(s + 1), s % 2, m8)

        for r in range(3):

            @pl.when(j == r)
            def _(r=r):
                send_o[h, r] = o.astype(jnp.bfloat16)
                send_t[h, r] = t
                start("O", r, h)
                start("T", r, h)

        @pl.when(j == 3)
        def _():
            part_o[h] = o
            part_t[h] = t

        return m8

    last = len(order) - 1
    m8 = lax.fori_loop(0, last, step, m8)
    o, t, _ = attend(order[last], None, last % 2, m8)
    part_o[nh - 1] = o
    part_t[nh - 1] = t
    finish(nh - 1)

    for h in range(nh):
        some = out.at[:, pl.ds(0, (uly - 1) * HD)]
        pltpu.make_async_copy(some, some, ao_r.at[h]).wait()
        pltpu.make_async_copy(some, some, ao_s.at[h]).wait()
        pltpu.make_async_copy(final.at[h, mine], out.at[:, out_columns(h)], lsem.at[9 + h]).wait()
    for n, dst in enumerate((qland, kland, vland)):
        whole = dst.at[pl.ds(0, (uly - 1) * rows)]
        pltpu.make_async_copy(whole, whole, a2a_s.at[n]).wait()
    pltpu.make_async_copy(kland, fresh.at[0], lsem.at[7]).wait()
    pltpu.make_async_copy(vland, fresh.at[1], lsem.at[8]).wait()
    for kind in KINDS:
        for h in range(nh):
            copy(kind, h).wait_send()


def local(queries, keys, values, stale_cache):
    rows, width = queries.shape
    _, patch_rows, cols = stale_cache.shape
    nh = cols // HD
    bf, f32 = jnp.bfloat16, jnp.float32
    n_copies = len(KINDS) * nh
    vm = pltpu.VMEM
    dma = pltpu.SemaphoreType.DMA
    return pl.pallas_call(
        kernel,
        out_shape=(
            jax.ShapeDtypeStruct((rows, width), bf),
            jax.ShapeDtypeStruct(stale_cache.shape, bf),
        ),
        in_specs=[pl.BlockSpec(memory_space=pl.ANY)] * 4,
        out_specs=(pl.BlockSpec(memory_space=pl.ANY),) * 2,
        scratch_shapes=[
            vm((9, nh, patch_rows, HD), bf),
            vm((9, nh, HD, patch_rows), bf),
            vm((4, nh, patch_rows, HD), bf),
            vm((patch_rows, cols), bf),
            vm((patch_rows, cols), bf),
            vm((patch_rows, cols), bf),
            vm((patch_rows, cols), bf),
            vm((2, 8 * patch_rows, patch_rows), f32),
            vm((nh, HD, patch_rows), f32),
            vm((nh, 8, patch_rows), f32),
            vm((nh, 3, HD, patch_rows), bf),
            vm((nh, 3, 8, patch_rows), f32),
            vm((nh, 3, HD, patch_rows), bf),
            vm((nh, 3, 8, patch_rows), f32),
            vm((nh, patch_rows, HD), bf),
            dma((n_copies,)),
            dma((n_copies,)),
            dma((3,)),
            dma((3,)),
            dma((nh,)),
            dma((nh,)),
            dma((9 + nh,)),
        ],
        compiler_params=pltpu.CompilerParams(
            collective_id=0, has_side_effects=True, vmem_limit_bytes=62 * 2**20
        ),
        cost_estimate=pl.CostEstimate(
            flops=4 * 8 * 4 * patch_rows**2 * cols,
            bytes_accessed=8 * patch_rows * cols,
            transcendentals=32 * patch_rows**2 * nh,
        ),
    )(queries, keys, values, stale_cache)


def solution(mesh):
    in_specs = (
        P(("patch", "uly"), None),
        P(("patch", "uly"), None),
        P(("patch", "uly"), None),
        P(None, "patch", "uly"),
    )
    out_specs = (P(("patch", "uly"), None), P(None, "patch", "uly"))
    return jax.shard_map(local, mesh=mesh, in_specs=in_specs, out_specs=out_specs, check_vma=False)
```

time: 81.1 us -> 68.6 us (0.85)
  Pallas kernels: 74 us -> 64.7 us
  local copies, waits for them, and re-layouts: 5.19 us -> 2.42 us
    pallas_call x1, Pallas kernels: 74 us -> 64.7 us  [local(): pl.pallas_call(kernel, out_shape=(jax.ShapeDtypeStruct((rows, width), bf)...]
    unnamed x10 -> x4, local copies, waits for them, and re-layouts: 5.19 us -> 2.42 us
where the time goes in v2:
time: 68.6 us; the launch traced here: 67.8 us
  Pallas kernels  64.7 us (94%)
  local copies, waits for them, and re-layouts  2.42 us (4%)
    pallas_call x1, Pallas kernels, local(): pl.pallas_call(kernel, out_shape=(jax.ShapeDtypeStruct((rows, width), bf)...  64.7 us
    unnamed x4, local copies, waits for them, and re-layouts  2.42 us

profile of v2, /device:TPU:6, one launch (start us, length us, event | category | flops | bytes accessed | tf_op | source)
XLA Modules:
  0.0 67.8 jit_solution(9931356372010226376)
XLA Ops:
  0.6 64.7 %shard_map.59 = (bf16[16,6144]{1,0:T(8,128)(2,1)}, bf16[2,256,384]{2,1,0:T(8,128)(2,1)}) custom-call(bf16[16,6144]{1,0:T(8,128)(2,1)} %q_hbm.1, bf16[16,6144]{1,0:T(8,128)(2,1)} %k_hbm.1, bf16[16,6144]{1,0:T(8,128)(2,1)} %v_hbm.1, bf16[2,256,384]{2,1,0:T(8,128)(2,1)} %stale.1), custom_call_target="tpu_custom_call" | custom-call | flops 3221225472 | bytes 786432 | tf_op jit(solution)/shard_map/pallas_call | solution.py:344
  65.4 0.0 copy-start
  65.4 1.7 %copy.8 = bf16[16,6144]{1,0:T(8,128)(2,1)} copy(bf16[16,6144]{1,0:T(8,128)(2,1)} %get-tuple-element.4) | data formatting | bytes 393216
  67.0 0.0 copy-done
  67.0 0.7 %copy.9 = bf16[2,256,384]{2,1,0:T(8,128)(2,1)} copy(bf16[2,256,384]{2,1,0:T(8,128)(2,1)S(1)} %copy-done) | data formatting | bytes 786432
Async XLA Ops:
  65.4 1.7 %copy-start = (bf16[2,256,384]{2,1,0:T(8,128)(2,1)S(1)}, bf16[2,256,384]{2,1,0:T(8,128)(2,1)}, u32[]{:S(2)}) copy-start(bf16[2,256,384]{2,1,0:T(8,128)(2,1)} %get-tuple-element.5) | copy-start | bytes 1179652

commit v3 on v2

--- a/solution.py
+++ b/solution.py
@@ -173,8 +173,6 @@
     start_query(0)
     start_query(1)
     start_query(2)
-    exchange(1, k_hbm, kland)
-    exchange(2, v_hbm, vland)
     for t in "KV":
         forward_xz(t, 0)
     start_both("x", 2)
@@ -225,10 +223,15 @@
 
     order = (
         (0, 1), (0, 2), (0, 0), (1, 1), (1, 2), (1, 0),
-        (0, 3), (2, 2), (2, 0), (1, 3), (2, 1), (2, 3),
+        (2, 2), (2, 0), (0, 3), (1, 3), (2, 1), (2, 3),
     )
     plan = {
-        0: lambda: (ready("V", 0), arrived("Q", "z", 0)),
+        0: lambda: (
+            ready("V", 0),
+            arrived("Q", "z", 0),
+            exchange(1, k_hbm, kland),
+            exchange(2, v_hbm, vland),
+        ),
         1: lambda: ([forward_z(t, 2) for t in "KV"], arrived("Q", "xz", 0)),
         2: lambda: (ready("K", 1), arrived("Q", "x", 1)),
         3: lambda: (
@@ -238,11 +241,10 @@
             arrived("Q", "z", 1),
         ),
         4: lambda: arrived("Q", "xz", 1),
-        5: take_fresh,
-        6: lambda: (ready("K", 2), arrived("Q", "z", 2)),
-        7: lambda: (ready("V", 2), arrived("Q", "xz", 2)),
-        8: lambda: finish(0),
-        9: lambda: arrived("Q", "x", 2),
+        5: lambda: (ready("K", 2), arrived("Q", "z", 2)),
+        6: lambda: (ready("V", 2), arrived("Q", "xz", 2)),
+        7: take_fresh,
+        9: lambda: (arrived("Q", "x", 2), finish(0)),
         10: lambda: finish(1),
     }
     blk = ka.shape[2]
@@ -333,6 +335,19 @@
             copy(kind, h).wait_send()
 
 
+def copy_out(*refs):
+    sems = refs[-1]
+    inward = [pltpu.make_async_copy(refs[i], refs[4 + i], sems.at[i]) for i in range(2)]
+    outward = [pltpu.make_async_copy(refs[4 + i], refs[2 + i], sems.at[2 + i]) for i in range(2)]
+    for c in inward:
+        c.start()
+    for c, d in zip(inward, outward):
+        c.wait()
+        d.start()
+    for d in outward:
+        d.wait()
+
+
 def local(queries, keys, values, stale_cache):
     rows, width = queries.shape
     _, patch_rows, cols = stale_cache.shape
@@ -341,7 +356,7 @@
     n_copies = len(KINDS) * nh
     vm = pltpu.VMEM
     dma = pltpu.SemaphoreType.DMA
-    return pl.pallas_call(
+    results = pl.pallas_call(
         kernel,
         out_shape=(
             jax.ShapeDtypeStruct((rows, width), bf),
@@ -382,6 +397,14 @@
             transcendentals=32 * patch_rows**2 * nh,
         ),
     )(queries, keys, values, stale_cache)
+    return pl.pallas_call(
+        copy_out,
+        out_shape=tuple(jax.ShapeDtypeStruct(r.shape, r.dtype) for r in results),
+        in_specs=[pl.BlockSpec(memory_space=pl.ANY)] * 2,
+        out_specs=(pl.BlockSpec(memory_space=pl.ANY),) * 2,
+        scratch_shapes=[vm(r.shape, r.dtype) for r in results] + [dma((4,))],
+        compiler_params=pltpu.CompilerParams(vmem_limit_bytes=62 * 2**20),
+    )(*results)
 
 
 def solution(mesh):

time: 68.6 us -> 64 us (0.933); the launches traced: 67.8 us -> 63.9 us
  local copies, waits for them, and re-layouts: 2.42 us -> 0 us
  Pallas kernels: 64.7 us -> 63.2 us
    pallas_call x1, Pallas kernels: 64.7 us -> 61.4 us  [local(): pl.pallas_call(kernel, out_shape=(jax.ShapeDtypeStruct((rows, width), bf)...]
    unnamed x4 -> x0, local copies, waits for them, and re-layouts: 2.42 us -> none
    pallas_call x0 -> x1, Pallas kernels: none -> 1.88 us  [local(): pl.pallas_call(copy_out, out_shape=tuple((jax.ShapeDtypeStruct(r.shape, r...]
where the time goes in v3:
time: 64 us; the launch traced here: 63.9 us
  Pallas kernels  63.2 us (99%)
  between operations  0.64 us (1%)
    pallas_call x1, Pallas kernels, local(): pl.pallas_call(kernel, out_shape=(jax.ShapeDtypeStruct((rows, width), bf)...  61.4 us
    pallas_call x1, Pallas kernels, local(): pl.pallas_call(copy_out, out_shape=tuple((jax.ShapeDtypeStruct(r.shape, r...  1.88 us

profile of v3, /device:TPU:6, one launch (start us, length us, event | category | flops | bytes accessed | tf_op | source)
XLA Modules:
  0.0 63.9 jit_solution(3922648189376305361)
XLA Ops:
  0.6 61.4 %shard_map.59 = (bf16[16,6144]{1,0:T(8,128)(2,1)}, bf16[2,256,384]{2,1,0:T(8,128)(2,1)}) custom-call(bf16[16,6144]{1,0:T(8,128)(2,1)} %q_hbm.1, bf16[16,6144]{1,0:T(8,128)(2,1)} %k_hbm.1, bf16[16,6144]{1,0:T(8,128)(2,1)} %v_hbm.1, bf16[2,256,384]{2,1,0:T(8,128)(2,1)} %stale.1), custom_call_target="tpu_custom_call" | custom-call | flops 3221225472 | bytes 786432 | tf_op jit(solution)/shard_map/pallas_call | solution.py:359
  62.0 1.9 %shard_map.60 = (bf16[16,6144]{1,0:T(8,128)(2,1)}, bf16[2,256,384]{2,1,0:T(8,128)(2,1)}) custom-call(bf16[16,6144]{1,0:T(8,128)(2,1)} %get-tuple-element.4.refs_0_, bf16[2,256,384]{2,1,0:T(8,128)(2,1)} %get-tuple-element.5.refs_1_), custom_call_target="tpu_custom_call" | custom-call | tf_op jit(solution)/shard_map/pallas_call | solution.py:400

commit v4 on v3

--- a/solution.py
+++ b/solution.py
@@ -223,7 +223,7 @@
 
     order = (
         (0, 1), (0, 2), (0, 0), (1, 1), (1, 2), (1, 0),
-        (2, 2), (2, 0), (0, 3), (1, 3), (2, 1), (2, 3),
+        (2, 2), (2, 0), (0, 3), (2, 1), (1, 3), (2, 3),
     )
     plan = {
         0: lambda: (
@@ -244,8 +244,8 @@
         5: lambda: (ready("K", 2), arrived("Q", "z", 2)),
         6: lambda: (ready("V", 2), arrived("Q", "xz", 2)),
         7: take_fresh,
-        9: lambda: (arrived("Q", "x", 2), finish(0)),
-        10: lambda: finish(1),
+        8: lambda: arrived("Q", "x", 2),
+        9: lambda: finish(0),
     }
     blk = ka.shape[2]
 
@@ -315,6 +315,7 @@
 
     last = len(order) - 1
     m8 = lax.fori_loop(0, last, step, m8)
+    finish(1)
     o, t, _ = attend(order[last], None, last % 2, m8)
     part_o[nh - 1] = o
     part_t[nh - 1] = t

time: 64 us -> 62.6 us (0.978)
  the two profiles are of different devices: /device:TPU:6 before, /device:TPU:1 now
where the time goes in v4:
time: 62.6 us; the launch traced here: 62.5 us
  Pallas kernels  61.9 us (99%)
  between operations  0.64 us (1%)
    pallas_call x1, Pallas kernels, local(): pl.pallas_call(kernel, out_shape=(jax.ShapeDtypeStruct((rows, width), bf)...  60 us
    pallas_call x1, Pallas kernels, local(): pl.pallas_call(copy_out, out_shape=tuple((jax.ShapeDtypeStruct(r.shape, r...  1.88 us

profile of v4, /device:TPU:1, one launch (start us, length us, event | category | flops | bytes accessed | tf_op | source)
XLA Modules:
  0.0 62.5 jit_solution(1322408521106016303)
XLA Ops:
  0.6 60.0 %shard_map.59 = (bf16[16,6144]{1,0:T(8,128)(2,1)}, bf16[2,256,384]{2,1,0:T(8,128)(2,1)}) custom-call(bf16[16,6144]{1,0:T(8,128)(2,1)} %q_hbm.1, bf16[16,6144]{1,0:T(8,128)(2,1)} %k_hbm.1, bf16[16,6144]{1,0:T(8,128)(2,1)} %v_hbm.1, bf16[2,256,384]{2,1,0:T(8,128)(2,1)} %stale.1), custom_call_target="tpu_custom_call" | custom-call | flops 3221225472 | bytes 786432 | tf_op jit(solution)/shard_map/pallas_call | solution.py:360
  60.6 1.9 %shard_map.60 = (bf16[16,6144]{1,0:T(8,128)(2,1)}, bf16[2,256,384]{2,1,0:T(8,128)(2,1)}) custom-call(bf16[16,6144]{1,0:T(8,128)(2,1)} %get-tuple-element.4.refs_0_, bf16[2,256,384]{2,1,0:T(8,128)(2,1)} %get-tuple-element.5.refs_1_), custom_call_target="tpu_custom_call" | custom-call | tf_op jit(solution)/shard_map/pallas_call | solution.py:401
